TPU v7x, 32 devices: a whole 2x2x4 slice. The times are simulated.
32 devices in a mesh: fsdp: 4 (over z), tensor: 8 (over y, x, core).
Axes of the slice: x: 2, y: 2, z: 4, core: 2. Of those that a mesh axis runs over, the one named last changes fastest.
Arguments:
- val_x: bfloat16 [2048, 8192], P('fsdp', 'tensor'), may hold values from -6 to 6
- val_cot: bfloat16 [2048, 16384], P('fsdp', 'tensor'), may hold values from -0.0014648438 to 0.0014648438
- second_moment: float32 [8192, 16384], P('fsdp', 'tensor'), may hold values from 0.01 to 1
- train_x: bfloat16 [1024, 8192], P('fsdp', 'tensor'), may hold values from -6 to 6
- train_cot: bfloat16 [1024, 16384], P('fsdp', 'tensor'), may hold values from -0.046875 to 0.046875
Outputs:
- scores: float32 [1024], P('fsdp')
All inputs are finite; a program needn't handle non-finite values.
Results may differ from a plain program's by a relative error of at most 0.019.
Values may be sent and summed in bfloat16 or wider, within the bound.
A program may use at most 128 MiB of HBM per device.

v0:
```python
import jax
import jax.numpy as jnp
from jax import lax
from jax.sharding import PartitionSpec as P

EPSILON = 1e-08


def per_device(val_x, val_cot, second_moment, train_x, train_cot):
    full_val = lax.all_gather(val_x, "tensor", axis=1, tiled=True)
    grad_rows = lax.psum_scatter(
        lax.dot_general(
            full_val, val_cot, (((0,), (0,)), ((), ())), preferred_element_type=jnp.float32
        ).astype(jnp.bfloat16),
        "fsdp",
        scatter_dimension=0,
        tiled=True,
    ).astype(jnp.float32)
    delta = (grad_rows / (jnp.sqrt(second_moment) + EPSILON)).astype(jnp.bfloat16)
    full_train = lax.all_gather(train_x, "tensor", axis=1, tiled=True)
    received = lax.all_to_all(full_train, "fsdp", split_axis=1, concat_axis=0, tiled=True)
    cot_whole = lax.all_gather(train_cot, "fsdp", axis=0, tiled=True)
    shifted = jnp.dot(received, delta, preferred_element_type=jnp.float32)
    block_scores = jnp.sum(shifted * cot_whole.astype(jnp.float32), axis=1)
    partial_scores = lax.psum_scatter(block_scores, "fsdp", scatter_dimension=0, tiled=True)
    return lax.psum(partial_scores, "tensor")


def solution(mesh):
    placed = (
        P("fsdp", "tensor"),
        P("fsdp", "tensor"),
        P("fsdp", "tensor"),
        P("fsdp", "tensor"),
        P("fsdp", "tensor"),
    )
    return jax.shard_map(
        per_device, mesh=mesh, in_specs=placed, out_specs=P("fsdp"), check_vma=False
    )
```

profile of v0, /device:TPU:0, one launch (start us, length us, event | category | flops | bytes accessed | tf_op | source)
XLA Modules:
  0.0 875.1 jit_solution(17885087888973293894)
XLA Ops:
  6.5 0.0 copy-start
  6.5 0.0 all-gather.4.cloned.1.call-start
  6.5 0.7 all-gather.4.cloned.1.call-update
  7.3 0.0 all-gather.6.cloned.1.call-start
  7.3 2.1 copy.11
  9.4 0.0 all-gather.6.cloned.1.call-update
  9.4 0.0 all-gather.8.cloned.1.call-start
  9.4 2.3 copy.13
  11.7 0.0 all-gather.8.cloned.1.call-update
  11.7 0.0 reduce-scatter.4.cloned.1.call-start
  11.8 54.6 %all-gather.4.cloned.1.call-done = bf16[512,8192]{1,0:T(8,128)(2,1)} async-done(((bf16[512,1024]{1,0:T(8,128)(2,1)}), bf16[512,8192]{1,0:T(8,128)(2,1)}) %all-gather.4.cloned.1.call-update) | async-done | bytes 8388624 | tf_op jit(solution)/shard_map/all_gather | solution.py:10
  66.4 25.2 %convolution_convert_fusion = bf16[8192,2048]{1,0:T(8,128)(2,1)} fusion(bf16[512,8192]{1,0:T(8,128)(2,1)} %all-gather.4.cloned.1.call-done, bf16[512,2048]{1,0:T(8,128)(2,1)S(1)} %copy-done), kind=kOutput, calls=%fused_computation | convolution fusion | flops 17196646400 | bytes 44040192 | tf_op jit(solution)/shard_map/dot_general | solution.py:12
  91.6 0.0 reduce-scatter.4.cloned.1.call-update
  91.6 0.0 copy-start.2
  91.6 13.4 %all-gather.6.cloned.1.call-done = bf16[256,8192]{0,1:T(8,128)(2,1)} async-done(((bf16[256,1024]{0,1:T(8,128)(2,1)}), bf16[256,8192]{0,1:T(8,128)(2,1)}) %all-gather.6.cloned.1.call-update) | async-done | bytes 4194320 | tf_op jit(solution)/shard_map/all_gather | solution.py:20
  105.0 4.8 all-to-all-start
  109.9 0.6 dynamic-slice
  111.1 160.1 %all-to-all-done = bf16[256,4,2048]{0,2,1:T(8,128)(2,1)} async-done(((bf16[256,4,2048]{0,2,1:T(8,128)(2,1)}), bf16[256,4,2048]{0,2,1:T(8,128)(2,1)}, u32[]{:S(2)}, u32[]{:S(2)}) %all-to-all-start) | async-done | bytes 4194336 | tf_op jit(solution)/shard_map/all_to_all | solution.py:21
  271.2 6.3 copy.12
  277.5 545.9 %reduce-scatter.4.cloned.1.call-done = bf16[2048,2048]{1,0:T(8,128)(2,1)} async-done(((bf16[8192,2048]{1,0:T(8,128)(2,1)}), bf16[2048,2048]{1,0:T(8,128)(2,1)}) %reduce-scatter.4.cloned.1.call-update) | async-done | bytes 8388624
  823.4 21.5 %fusion = f32[1024]{0:T(1024)S(1)} fusion(bf16[1024,2048]{0,1:T(8,128)(2,1)} %all-gather.8.cloned.1.call-done, bf16[1024,2048]{1,0:T(8,128)(2,1)} %bitcast.12, f32[2048,2048]{1,0:T(8,128)} %param.7, bf16[2048,2048]{1,0:T(8,128)(2,1)} %reduce-scatter.4.cloned.1.call-done), kind=kOutput, calls=%fused_computation.3 | convolution fusion | flops 8613002240 | bytes 33558528 | tf_op jit(solution)/shard_map/dot_general | solution.py:23
  844.9 11.2 %all-reduce.1 = f32[1024]{0:T(1024)S(1)} all-reduce(f32[1024]{0:T(1024)S(1)} %fusion), channel_id=3, replica_groups=mesh['fsdp'=4,'tensor'=8] {'fsdp'}, use_global_device_ids=true, to_apply=%region_2.0.clone | all-reduce | flops 1024 | bytes 8192
  856.1 0.1 dynamic-slice.3
  856.1 12.4 %psum.7 = f32[256]{0:T(256)} all-reduce(f32[256]{0:T(256)S(1)} %dynamic-slice.3), channel_id=1, replica_groups=mesh['fsdp'=4,'tensor'=8] {'tensor'}, use_global_device_ids=true, to_apply=%region_3.0 | all-reduce | flops 256 | bytes 2048 | tf_op jit(solution)/shard_map/psum | solution.py:26
  (5 shorter events, 0.0 us)
Async XLA Ops:
  6.5 59.9 %copy-start = (bf16[512,2048]{1,0:T(8,128)(2,1)S(1)}, bf16[512,2048]{1,0:T(8,128)(2,1)}, u32[]{:S(2)}) copy-start(bf16[512,2048]{1,0:T(8,128)(2,1)} %param.6) | copy-start | bytes 6291460
  6.5 59.9 %all-gather.4.cloned.1.call-start = ((), (), s32[]{:S(2)}) async-start(), calls=%async_computation.2 | async-start | bytes 9437184 | tf_op jit(solution)/shard_map/all_gather | solution.py:10
  7.3 97.8 %all-gather.6.cloned.1.call-start = ((), (), s32[]{:S(2)}) async-start(), calls=%async_computation.3 | async-start | bytes 4718592 | tf_op jit(solution)/shard_map/all_gather | solution.py:20
  9.4 268.1 %all-gather.8.cloned.1.call-start = ((), (), s32[]{:S(2)}) async-start(), calls=%async_computation.4 | async-start | bytes 5242880 | tf_op jit(solution)/shard_map/all_gather | solution.py:22
  11.7 811.6 %reduce-scatter.4.cloned.1.call-start = ((), (), s32[]{:S(2)}) async-start(), calls=%async_computation.5 | async-start | bytes 41943040
  91.6 18.3 %copy-start.2 = (u32[32]{0:T(128)S(1)}, u32[32]{0:T(128)}, u32[]{:S(2)}) copy-start(u32[32]{0:T(128)} %constant.6) | copy-start | bytes 388
  105.0 166.2 %all-to-all-start = ((bf16[256,4,2048]{0,2,1:T(8,128)(2,1)}), bf16[256,4,2048]{0,2,1:T(8,128)(2,1)}, u32[]{:S(2)}, u32[]{:S(2)}) async-start(bf16[256,4,2048]{0,2,1:T(8,128)(2,1)} %bitcast.11), calls=%async_computation | async-start | bytes 8388608 | tf_op jit(solution)/shard_map/all_to_all | solution.py:21
  823.4 45.2 %copy-start.1 = (bf16[512,2048]{1,0:T(8,128)(2,1)S(1)}, bf16[512,2048]{1,0:T(8,128)(2,1)}, u32[]{:S(2)}) copy-start(bf16[512,2048]{1,0:T(8,128)(2,1)} %param.6) | copy-start | bytes 6291460
Sparse Core Ops, SparseCore 0:
  9.3 57.0 all-gather.3
  68.3 36.7 all-gather.5
  106.6 154.4 all-gather.7
  263.3 560.0 reduce-scatter.3
where the time goes:
time: 876 us; the launch traced here: 875 us
  waiting for transfers between devices  775 us (88%)
  matrix products  46.7 us (5%)
  blocking collectives  23.6 us (3%)
  between operations  13.8 us (2%)
  local copies, waits for them, and re-layouts  11.3 us (1%)
    unnamed x5, waiting for transfers between devices  547 us
    all_to_all x1, waiting for transfers between devices, per_device(): lax.all_to_all(full_train, 'fsdp', split_axis=1, concat_axis=0, tiled=True)  160 us
    all_gather x1, waiting for transfers between devices, per_device(): full_val = lax.all_gather(val_x, 'tensor', axis=1, tiled=True)  54.6 us
    dot_general x1, matrix products, per_device(): lax.dot_general(full_val, val_cot, (((0,), (0,)), ((), ())), preferred_el...  25.2 us
    dot_general x1, matrix products, per_device(): shifted = jnp.dot(received, delta, preferred_element_type=jnp.float32)  21.5 us
  transfers between devices with their start and end apart: 5, of which 4 were waited for; matrix products, arithmetic and copies ran while one was open for 4% of the time, Pallas kernels for 0%

commit v1 on v0

v1 whole, which is shorter than its diff:
```python
import jax
import jax.numpy as jnp
from jax import lax
from jax.sharding import PartitionSpec as P

EPSILON = 1e-08


def rows_of_block(x):
    n_tensor, n_fsdp = lax.axis_size("tensor"), lax.axis_size("fsdp")
    share = x.shape[0] // n_tensor
    spread = lax.all_to_all(x, "tensor", split_axis=0, concat_axis=1, tiled=True)
    moved = lax.all_to_all(spread, "fsdp", split_axis=1, concat_axis=0, tiled=True)
    whole = lax.all_gather(moved, "tensor", axis=0, tiled=True)
    rows = whole.shape[1]
    whole = whole.reshape(n_tensor, n_fsdp, share, rows)
    return whole.transpose(1, 0, 2, 3).reshape(n_fsdp * n_tensor * share, rows)


def per_device(val_x, val_cot, second_moment, train_x, train_cot):
    all_cot = lax.all_gather(val_cot, "fsdp", axis=0, tiled=True)
    all_train_cot = lax.all_gather(train_cot, "fsdp", axis=0, tiled=True)
    x_rows = rows_of_block(val_x)
    train_rows = rows_of_block(train_x)
    grad = lax.dot_general(
        x_rows, all_cot, (((0,), (0,)), ((), ())), preferred_element_type=jnp.float32
    )
    delta = (grad / (jnp.sqrt(second_moment) + EPSILON)).astype(jnp.bfloat16)
    shifted = jnp.dot(train_rows, delta, preferred_element_type=jnp.float32)
    block_scores = jnp.sum(shifted * all_train_cot.astype(jnp.float32), axis=1)
    partial_scores = lax.psum_scatter(block_scores, "fsdp", scatter_dimension=0, tiled=True)
    return lax.psum(partial_scores, "tensor")


def solution(mesh):
    return jax.shard_map(
        per_device,
        mesh=mesh,
        in_specs=(P("fsdp", "tensor"),) * 5,
        out_specs=P("fsdp"),
        check_vma=False,
    )
```

time: 876 us -> 446 us (0.51)
  waiting for transfers between devices: 775 us -> 267 us
  blocking collectives: 23.6 us -> 108 us
    unnamed x5 -> x4, waiting for transfers between devices: 547 us -> 0.39 us
    all_gather x3 -> x4, waiting for transfers between devices: 68 us -> 267 us  [the longest x1 149 us: per_device(): all_cot = lax.all_gather(val_cot, 'fsdp', axis=0, tiled=True)]
    all_to_all x1 -> x0, waiting for transfers between devices: 160 us -> none  [per_device(): lax.all_to_all(full_train, 'fsdp', split_axis=1, concat_axis=0, tiled=True)]
    all_to_all x0 -> x4, blocking collectives: none -> 86.5 us  [the longest x2 47.1 us: rows_of_block(): lax.all_to_all(spread, 'fsdp', split_axis=1, concat_axis=0, tiled=True)]
    reshape x0 -> x2, local copies, waits for them, and re-layouts: none -> 13.5 us  [rows_of_block(): whole = whole.reshape(n_tensor, n_fsdp, share, rows)]
    dot_general x2 -> x1, matrix products: 46.7 us -> 38 us  [per_device(): shifted = jnp.dot(train_rows, delta, preferred_element_type=jnp.float32)]
  transfers between devices with their start and end apart: 5 -> 4, of which waited for: 4 -> 3; matrix products, arithmetic and copies ran while one was open for 4% -> 4% of each run, Pallas kernels for 0% -> 0%
where the time goes in v1:
time: 446 us; the launch traced here: 445 us
  waiting for transfers between devices  267 us (60%)
  blocking collectives  108 us (24%)
  matrix products  38 us (9%)
  local copies, waits for them, and re-layouts  18.5 us (4%)
  between operations  13.9 us (3%)
    all_gather x1, waiting for transfers between devices, per_device(): all_cot = lax.all_gather(val_cot, 'fsdp', axis=0, tiled=True)  149 us
    all_gather x1, waiting for transfers between devices, per_device(): all_train_cot = lax.all_gather(train_cot, 'fsdp', axis=0, tiled=True)  73.9 us
    all_to_all x2, blocking collectives, rows_of_block(): lax.all_to_all(spread, 'fsdp', split_axis=1, concat_axis=0, tiled=True)  47.1 us
    all_gather x2, waiting for transfers between devices, rows_of_block(): whole = lax.all_gather(moved, 'tensor', axis=0, tiled=True)  43.4 us
    all_to_all x2, blocking collectives, rows_of_block(): lax.all_to_all(x, 'tensor', split_axis=0, concat_axis=1, tiled=True)  39.4 us
    dot_general x1, matrix products, per_device(): shifted = jnp.dot(train_rows, delta, preferred_element_type=jnp.float32)  38 us
    reshape x2, local copies, waits for them, and re-layouts, rows_of_block(): whole = whole.reshape(n_tensor, n_fsdp, share, rows)  13.5 us
    psum x1, blocking collectives, per_device(): return lax.psum(partial_scores, 'tensor')  12.6 us
  transfers between devices with their start and end apart: 4, of which 3 were waited for; matrix products, arithmetic and copies ran while one was open for 4% of the time, Pallas kernels for 0%

profile of v1, /device:TPU:0, one launch (start us, length us, event | category | flops | bytes accessed | tf_op | source)
XLA Modules:
  0.0 445.3 jit_solution(10117382803456505181)
XLA Ops:
  6.5 14.9 %all_to_all.70 = bf16[8,32,1024]{2,1,0:T(8,128)(2,1)S(1)} all-to-all(bf16[8,32,1024]{2,1,0:T(8,128)(2,1)} %bitcast.35), channel_id=1, replica_groups=mesh['fsdp'=4,'tensor'=8] {'tensor'}, dimensions={0} | all-to-all | bytes 1048576 | tf_op jit(solution)/shard_map/all_to_all | solution.py:12
  21.5 0.3 copy.17
  21.7 0.4 all_to_all.62
  22.1 0.3 copy.18
  22.4 18.6 %all_to_all.71 = bf16[32,4,2048]{2,0,1:T(8,128)(2,1)} all-to-all(bf16[32,4,2048]{2,0,1:T(8,128)(2,1)S(1)} %copy.18), channel_id=1, replica_groups=mesh['fsdp'=4,'tensor'=8] {'fsdp'}, dimensions={1} | all-to-all | bytes 1048576 | tf_op jit(solution)/shard_map/all_to_all | solution.py:13
  41.1 24.5 %all_to_all.72 = bf16[8,64,1024]{2,1,0:T(8,128)(2,1)S(1)} all-to-all(bf16[8,64,1024]{2,1,0:T(8,128)(2,1)} %bitcast.34), channel_id=1, replica_groups=mesh['fsdp'=4,'tensor'=8] {'tensor'}, dimensions={0} | all-to-all | bytes 2097152 | tf_op jit(solution)/shard_map/all_to_all | solution.py:12
  65.6 0.6 copy.14
  66.2 0.8 all_to_all.55
  67.0 0.6 copy.15
  67.6 28.5 %all_to_all.73 = bf16[64,4,2048]{2,0,1:T(8,128)(2,1)} all-to-all(bf16[64,4,2048]{2,0,1:T(8,128)(2,1)S(1)} %copy.15), channel_id=1, replica_groups=mesh['fsdp'=4,'tensor'=8] {'fsdp'}, dimensions={1} | all-to-all | bytes 2097152 | tf_op jit(solution)/shard_map/all_to_all | solution.py:13
  96.1 0.0 all-gather.11.cloned.1.call-start
  96.2 1.3 copy.20
  97.5 0.2 all-gather.7.cloned.1.call-start
  97.8 0.3 all-gather.7.cloned.1.call-update
  98.1 0.6 dynamic-slice
  99.4 5.2 %copy.19 = bf16[8,4,32,2048]{3,2,0,1:T(8,128)(2,1)} copy(bf16[8,4,32,2048]{3,2,1,0:T(8,128)(2,1)} %bitcast.28) | data formatting | bytes 8388608 | tf_op jit(solution)/shard_map/reshape | solution.py:16
  104.6 43.4 %all-gather.5.cloned.1.call-done = bf16[2048,2048]{1,0:T(8,128)(2,1)} async-done(((bf16[256,2048]{1,0:T(8,128)(2,1)}), bf16[2048,2048]{1,0:T(8,128)(2,1)}) %all-gather.5.cloned.1.call-update) | async-done | bytes 8388624 | tf_op jit(solution)/shard_map/all_gather | solution.py:14
  148.0 8.3 %copy.16 = bf16[8,4,64,2048]{3,2,0,1:T(8,128)(2,1)} copy(bf16[8,4,64,2048]{3,2,1,0:T(8,128)(2,1)} %bitcast.26) | data formatting | bytes 16777216 | tf_op jit(solution)/shard_map/reshape | solution.py:16
  156.3 73.9 %all-gather.11.cloned.1.call-done = bf16[1024,2048]{0,1:T(8,128)(2,1)} async-done(((bf16[256,2048]{0,1:T(8,128)(2,1)}), bf16[1024,2048]{0,1:T(8,128)(2,1)}) %all-gather.11.cloned.1.call-update) | async-done | bytes 4194320 | tf_op jit(solution)/shard_map/all_gather | solution.py:22
  230.1 149.3 %all-gather.7.cloned.1.call-done = bf16[2048,2048]{1,0:T(8,128)(2,1)} async-done(((bf16[512,2048]{1,0:T(8,128)(2,1)}), bf16[2048,2048]{1,0:T(8,128)(2,1)}) %all-gather.7.cloned.1.call-update) | async-done | bytes 8388624 | tf_op jit(solution)/shard_map/all_gather | solution.py:21
  379.4 38.0 %fusion = f32[1024]{0:T(1024)S(1)} fusion(bf16[1024,2048]{0,1:T(8,128)(2,1)} %all-gather.11.cloned.1.call-done, bf16[1024,2048]{1,0:T(8,128)(2,1)} %bitcast.29, f32[2048,2048]{1,0:T(8,128)} %param.7, bf16[2048,2048]{1,0:T(8,128)(2,1)} %bitcast.27, bf16[2048,2048]{1,0:T(8,128)(2,1)} %all-gather.7.cloned.1.call-done), kind=kOutput, calls=%fused_computation.2 | convolution fusion | flops 25788678144 | bytes 41947136 | tf_op jit(solution)/shard_map/dot_general | solution.py:29
  417.4 8.7 %all-reduce = f32[1024]{0:T(1024)S(1)} all-reduce(f32[1024]{0:T(1024)S(1)} %fusion), channel_id=2, replica_groups=mesh['fsdp'=4,'tensor'=8] {'fsdp'}, use_global_device_ids=true, to_apply=%region_1.0.clone | all-reduce | flops 1024 | bytes 8192
  426.1 0.1 dynamic-slice.1
  426.2 12.6 %psum.7 = f32[256]{0:T(256)} all-reduce(f32[256]{0:T(256)S(1)} %dynamic-slice.1), channel_id=1, replica_groups=mesh['fsdp'=4,'tensor'=8] {'tensor'}, use_global_device_ids=true, to_apply=%region_2.0 | all-reduce | flops 256 | bytes 2048 | tf_op jit(solution)/shard_map/psum | solution.py:32
  (10 shorter events, 0.1 us)
Async XLA Ops:
  6.5 92.8 %all-gather.9.cloned.1.call-start = ((), (), s32[]{:S(2)}) async-start(), calls=%async_computation.6 | async-start | bytes 4718592 | tf_op jit(solution)/shard_map/all_gather | solution.py:14
  21.4 74.7 %copy-start = (bf16[256,2048]{1,0:T(8,128)(2,1)S(1)}, bf16[256,2048]{1,0:T(8,128)(2,1)}, u32[]{:S(2)}) copy-start(bf16[256,2048]{1,0:T(8,128)(2,1)} %param.9) | copy-start | bytes 3145732
  41.1 106.9 %all-gather.5.cloned.1.call-start = ((), (), s32[]{:S(2)}) async-start(), calls=%async_computation.4 | async-start | bytes 9437184 | tf_op jit(solution)/shard_map/all_gather | solution.py:14
  41.1 57.0 %copy-start.1 = (u32[32]{0:T(128)S(1)}, u32[32]{0:T(128)}, u32[]{:S(2)}) copy-start(u32[32]{0:T(128)} %constant.6) | copy-start | bytes 388
  96.1 134.0 %all-gather.11.cloned.1.call-start = ((), (), s32[]{:S(2)}) async-start(), calls=%async_computation.7 | async-start | bytes 5242880 | tf_op jit(solution)/shard_map/all_gather | solution.py:22
  97.5 281.9 %all-gather.7.cloned.1.call-start = ((), (), s32[]{:S(2)}) async-start(), calls=%async_computation.5 | async-start | bytes 10485760 | tf_op jit(solution)/shard_map/all_gather | solution.py:21
Sparse Core Ops, SparseCore 0:
  41.2 42.1 all-gather.8
  96.2 51.7 all-gather.4
  149.5 80.5 all-gather.10
  231.6 147.8 all-gather.6

commit v2 on v1

v2 whole, which is shorter than its diff:
```python
import functools

import jax
import jax.numpy as jnp
from jax import lax
from jax.experimental import pallas as pl
from jax.experimental.pallas import tpu as pltpu
from jax.sharding import PartitionSpec as P

EPSILON = 1e-08
CHUNK = 256
MESH = pl.DeviceIdType.MESH


def kernel(
    n_fsdp, n_tensor,
    val_x, val_cot, moment, train_x, train_cot, out,
    spread, spread_t, x_all, t_all, x_turned, cot, cot_t, moment_v, shifted, total,
    part, first, second,
    a_send, a_recv, b_send, b_recv, c_send, c_recv, up_send, down_send, cot_recv,
    moment_sem, own_sem, local_sem, r1_send, r1_recv, r2_send, r2_recv,
):
    z, t = lax.axis_index("fsdp"), lax.axis_index("tensor")
    chunks = cot.shape[0]
    depth, depth_t = val_cot.shape[0], train_cot.shape[0]
    rows, features = moment.shape[0], val_x.shape[1]
    share, share_t = spread.shape[0], spread_t.shape[0]

    def on_tensor(d):
        return lax.rem(t + d, n_tensor)

    def on_fsdp(d):
        return lax.rem(z + d, n_fsdp)

    def remote(src, dst, send, recv, device):
        return pltpu.make_async_remote_copy(
            src_ref=src, dst_ref=dst, send_sem=send, recv_sem=recv,
            device_id=device, device_id_type=MESH,
        )

    def loop(low, high, body):
        def step(i, carry):
            body(i)
            return carry
        lax.fori_loop(low, high, step, 0)

    barrier = pltpu.get_barrier_semaphore()

    @functools.partial(loop, 1, n_tensor)
    def _(d):
        pl.semaphore_signal(barrier, 1, device_id={"tensor": on_tensor(d)}, device_id_type=MESH)

    @functools.partial(loop, 1, n_fsdp)
    def _(d):
        pl.semaphore_signal(barrier, 1, device_id={"fsdp": on_fsdp(d)}, device_id_type=MESH)

    pl.semaphore_wait(barrier, n_tensor + n_fsdp - 2)

    def a_copies(peer, owner, d):
        columns = pl.ds(pl.multiple_of(owner * features, features), features)
        return (
            remote(val_x.at[pl.ds(pl.multiple_of(peer * share, share), share)],
                   spread.at[:, columns], a_send.at[0, d], a_recv.at[0, owner], {"tensor": peer}),
            remote(train_x.at[pl.ds(pl.multiple_of(peer * share_t, share_t), share_t)],
                   spread_t.at[:, columns], a_send.at[1, d], a_recv.at[1, owner], {"tensor": peer}),
        )

    def a_own():
        columns = pl.ds(pl.multiple_of(t * features, features), features)
        return (
            pltpu.make_async_copy(val_x.at[pl.ds(pl.multiple_of(t * share, share), share)],
                                  spread.at[:, columns], local_sem.at[0]),
            pltpu.make_async_copy(train_x.at[pl.ds(pl.multiple_of(t * share_t, share_t), share_t)],
                                  spread_t.at[:, columns], local_sem.at[1]),
        )

    def b_copies(peer, owner, d):
        columns = pl.ds(pl.multiple_of(peer * rows, rows), rows)
        return (
            remote(spread.at[:, columns],
                   x_all.at[owner, pl.ds(pl.multiple_of(t * share, share), share)],
                   b_send.at[0, d], b_recv.at[0, owner], {"fsdp": peer}),
            remote(spread_t.at[:, columns],
                   t_all.at[owner, pl.ds(pl.multiple_of(t * share_t, share_t), share_t)],
                   b_send.at[1, d], b_recv.at[1, owner], {"fsdp": peer}),
        )

    def b_own():
        columns = pl.ds(pl.multiple_of(z * rows, rows), rows)
        return (
            pltpu.make_async_copy(
                spread.at[:, columns],
                x_all.at[z, pl.ds(pl.multiple_of(t * share, share), share)], local_sem.at[0]),
            pltpu.make_async_copy(
                spread_t.at[:, columns],
                t_all.at[z, pl.ds(pl.multiple_of(t * share_t, share_t), share_t)],
                local_sem.at[1]),
        )

    def c_copies(peer, owner, d):
        piece = pl.ds(pl.multiple_of(owner * share, share), share)
        piece_t = pl.ds(pl.multiple_of(owner * share_t, share_t), share_t)
        return (
            remote(x_all.at[:, piece], x_all.at[:, piece],
                   c_send.at[0, d], c_recv.at[0, owner], {"tensor": peer}),
            remote(t_all.at[:, piece_t], t_all.at[:, piece_t],
                   c_send.at[1, d], c_recv.at[1, owner], {"tensor": peer}),
        )

    def cot_places(shard, c):
        return (cot.at[c, pl.ds(pl.multiple_of(shard * depth, depth), depth)],
                cot_t.at[c, pl.ds(pl.multiple_of(shard * depth_t, depth_t), depth_t)])

    def cot_copies(shard, c, sems, peer, own):
        places = cot_places(shard, c)
        columns = pl.ds(pl.multiple_of(c * CHUNK, CHUNK), CHUNK)
        sources = (val_cot.at[:, columns], train_cot.at[:, columns]) if own else places
        return tuple(
            remote(sources[i], places[i], sems.at[i, shard, c], cot_recv.at[i, shard, c],
                   {"fsdp": peer})
            for i in range(2)
        )

    below, above = lax.max(z - 1, 0), lax.min(z + 1, n_fsdp - 1)

    def start_cot(shard, c, own):
        @pl.when(z < n_fsdp - 1)
        def _():
            if own:
                for copy in cot_copies(shard, c, up_send, above, own):
                    copy.start()
        @pl.when(z > 0)
        def _():
            if own:
                for copy in cot_copies(shard, c, down_send, below, own):
                    copy.start()

    def cot_own(c):
        columns = pl.ds(pl.multiple_of(c * CHUNK, CHUNK), CHUNK)
        places = cot_places(z, c)
        return (
            pltpu.make_async_copy(val_cot.at[:, columns], places[0], own_sem.at[0, c]),
            pltpu.make_async_copy(train_cot.at[:, columns], places[1], own_sem.at[1, c]),
        )

    def moment_copy(c):
        columns = pl.ds(pl.multiple_of(c * CHUNK, CHUNK), CHUNK)
        return pltpu.make_async_copy(moment.at[:, columns], moment_v.at[c], moment_sem.at[c])

    @functools.partial(loop, 1, n_tensor)
    def _(d):
        for copy in a_copies(on_tensor(d), t, d):
            copy.start()

    for copy in a_own():
        copy.start()
    early = 1
    loop(0, early, lambda c: start_cot(z, c, True))

    @functools.partial(loop, 1, n_tensor)
    def _(d):
        owner = on_tensor(d)
        for copy in a_copies(owner, owner, d):
            copy.wait_recv()

    for copy in a_own():
        copy.wait()

    @functools.partial(loop, 1, n_fsdp)
    def _(d):
        for copy in b_copies(on_fsdp(d), z, d):
            copy.start()

    for copy in b_own():
        copy.start()
    loop(early, chunks, lambda c: start_cot(z, c, True))

    @functools.partial(loop, 0, chunks)
    def _(c):
        for copy in cot_own(c):
            copy.start()
        moment_copy(c).start()

    @functools.partial(loop, 1, n_fsdp)
    def _(d):
        owner = on_fsdp(d)
        for copy in b_copies(owner, owner, d):
            copy.wait_recv()

    for copy in b_own():
        copy.wait()

    @functools.partial(loop, 1, n_tensor)
    def _(d):
        for copy in c_copies(on_tensor(d), t, d):
            copy.start()

    def pass_on(k, c):
        lower, upper = z - k, z + k

        @pl.when(lower >= 0)
        def _():
            copies = cot_copies(lower, c, up_send, above, False)
            for copy in copies:
                copy.wait_recv()

            @pl.when(z < n_fsdp - 1)
            def _():
                for copy in copies:
                    copy.start()

        @pl.when(upper < n_fsdp)
        def _():
            copies = cot_copies(upper, c, down_send, below, False)
            for copy in copies:
                copy.wait_recv()

            @pl.when(z > 0)
            def _():
                for copy in copies:
                    copy.start()

    @functools.partial(loop, 1, n_fsdp - 1)
    def _(k):
        loop(0, chunks, lambda c: pass_on(k, c))

    @functools.partial(loop, 1, n_tensor)
    def _(d):
        owner = on_tensor(d)
        for copy in c_copies(owner, owner, d):
            copy.wait_recv()

    tile = 256

    @functools.partial(loop, 0, rows // tile)
    def _(i):
        columns = pl.ds(pl.multiple_of(i * tile, tile), tile)
        for group in range(n_fsdp):
            x_turned[columns, group * depth:(group + 1) * depth] = x_all[group, :, columns].T

    total[...] = jnp.zeros_like(total)

    @functools.partial(loop, 0, chunks)
    def _(c):
        pass_on(n_fsdp - 1, c)
        for copy in cot_own(c):
            copy.wait()
        moment_copy(c).wait()
        shifted[...] = jnp.zeros_like(shifted)

        @functools.partial(loop, 0, rows // tile)
        def _(i):
            block = pl.ds(pl.multiple_of(i * tile, tile), tile)
            grad = jnp.dot(x_turned[block, :], cot[c], preferred_element_type=jnp.float32)
            delta = (grad / (jnp.sqrt(moment_v[c, block, :]) + EPSILON)).astype(jnp.bfloat16)
            lhs = t_all[:, :, block].reshape(n_fsdp * depth_t, tile)
            shifted[...] += jnp.dot(lhs, delta, preferred_element_type=jnp.float32)

        scored = shifted[...] * cot_t[c].astype(jnp.float32)
        folded = scored[:, :128]
        for low in range(128, CHUNK, 128):
            folded = folded + scored[:, low:low + 128]
        total[...] += folded

    for block in range(n_fsdp):
        turned = total[block * depth_t:(block + 1) * depth_t, :].T
        part[block] = jnp.sum(turned.reshape(16, 8, depth_t), axis=0)

    def r1_copy(peer, owner, d):
        return remote(part.at[peer], first.at[owner], r1_send.at[d], r1_recv.at[owner],
                      {"fsdp": peer})

    @functools.partial(loop, 1, n_fsdp)
    def _(d):
        r1_copy(on_fsdp(d), z, d).start()

    first[z] = part[z]

    @functools.partial(loop, 1, n_fsdp)
    def _(d):
        owner = on_fsdp(d)
        r1_copy(owner, owner, d).wait_recv()

    second[t] = jnp.sum(first[...], axis=0)

    def r2_copy(peer, owner, d):
        return remote(second.at[owner], second.at[owner], r2_send.at[d], r2_recv.at[owner],
                      {"tensor": peer})

    @functools.partial(loop, 1, n_tensor)
    def _(d):
        r2_copy(on_tensor(d), t, d).start()

    @functools.partial(loop, 1, n_tensor)
    def _(d):
        owner = on_tensor(d)
        r2_copy(owner, owner, d).wait_recv()

    out[...] = jnp.sum(jnp.sum(second[...], axis=0), axis=0, keepdims=True)

    @functools.partial(loop, 1, n_tensor)
    def _(d):
        peer = on_tensor(d)
        for copy in a_copies(peer, t, d) + c_copies(peer, t, d) + (r2_copy(peer, t, d),):
            copy.wait_send()

    @functools.partial(loop, 1, n_fsdp)
    def _(d):
        peer = on_fsdp(d)
        for copy in b_copies(peer, z, d) + (r1_copy(peer, z, d),):
            copy.wait_send()

    @functools.partial(loop, 0, n_fsdp)
    def _(shard):
        @pl.when((shard <= z) & (z < n_fsdp - 1))
        def _():
            @functools.partial(loop, 0, chunks)
            def _(c):
                for copy in cot_copies(shard, c, up_send, above, False):
                    copy.wait_send()

        @pl.when((shard >= z) & (z > 0))
        def _():
            @functools.partial(loop, 0, chunks)
            def _(c):
                for copy in cot_copies(shard, c, down_send, below, False):
                    copy.wait_send()


def per_device(n_fsdp, n_tensor, val_x, val_cot, second_moment, train_x, train_cot):
    depth, depth_t = val_x.shape[0], train_x.shape[0]
    rows, hidden = second_moment.shape
    chunks = hidden // CHUNK
    width = val_x.shape[1] * n_tensor
    bf16, f32 = jnp.bfloat16, jnp.float32
    dma = pltpu.SemaphoreType.DMA
    scores = pl.pallas_call(
        functools.partial(kernel, n_fsdp, n_tensor),
        out_shape=jax.ShapeDtypeStruct((1, depth_t), f32),
        in_specs=[pl.BlockSpec(memory_space=pl.ANY)] * 5,
        out_specs=pl.BlockSpec(memory_space=pltpu.VMEM),
        scratch_shapes=[
            pltpu.VMEM((depth // n_tensor, width), bf16),
            pltpu.VMEM((depth_t // n_tensor, width), bf16),
            pltpu.VMEM((n_fsdp, depth, rows), bf16),
            pltpu.VMEM((n_fsdp, depth_t, rows), bf16),
            pltpu.VMEM((rows, n_fsdp * depth), bf16),
            pltpu.VMEM((chunks, n_fsdp * depth, CHUNK), bf16),
            pltpu.VMEM((chunks, n_fsdp * depth_t, CHUNK), bf16),
            pltpu.VMEM((chunks, rows, CHUNK), f32),
            pltpu.VMEM((n_fsdp * depth_t, CHUNK), f32),
            pltpu.VMEM((n_fsdp * depth_t, 128), f32),
            pltpu.VMEM((n_fsdp, 8, depth_t), f32),
            pltpu.VMEM((n_fsdp, 8, depth_t), f32),
            pltpu.VMEM((n_tensor, 8, depth_t), f32),
            dma((2, n_tensor)), dma((2, n_tensor)),
            dma((2, n_fsdp)), dma((2, n_fsdp)),
            dma((2, n_tensor)), dma((2, n_tensor)),
            dma((2, n_fsdp, chunks)), dma((2, n_fsdp, chunks)), dma((2, n_fsdp, chunks)),
            dma((chunks,)), dma((2, chunks)), dma((2,)),
            dma((n_fsdp,)), dma((n_fsdp,)), dma((n_tensor,)), dma((n_tensor,)),
        ],
        compiler_params=pltpu.CompilerParams(
            collective_id=0, has_side_effects=True, vmem_limit_bytes=60 * 1024 * 1024
        ),
        name="scores",
    )(val_x, val_cot, second_moment, train_x, train_cot)
    return scores.reshape(depth_t)


def solution(mesh):
    return jax.shard_map(
        functools.partial(per_device, mesh.shape["fsdp"], mesh.shape["tensor"]),
        mesh=mesh,
        in_specs=(P("fsdp", "tensor"),) * 5,
        out_specs=P("fsdp"),
        check_vma=False,
    )
```

time: 446 us -> 268 us (0.60)
  Pallas kernels: 0 us -> 267 us
  waiting for transfers between devices: 267 us -> 0 us
  blocking collectives: 108 us -> 0 us
  matrix products: 38 us -> 0 us
  local copies, waits for them, and re-layouts: 18.5 us -> 1.24 us
  between operations: 13.9 us -> 0.01 us
    pallas_call x0 -> x1, Pallas kernels: none -> 267 us  [per_device(): pl.pallas_call(functools.partial(kernel, n_fsdp, n_tensor), out_shape=jax...]
    all_gather x4 -> x0, waiting for transfers between devices: 267 us -> none  [the longest x1 149 us: per_device(): all_cot = lax.all_gather(val_cot, 'fsdp', axis=0, tiled=True)]
    all_to_all x4 -> x0, blocking collectives: 86.5 us -> none  [the longest x2 47.1 us: rows_of_block(): lax.all_to_all(spread, 'fsdp', split_axis=1, concat_axis=0, tiled=True)]
    dot_general x1 -> x0, matrix products: 38 us -> none  [per_device(): shifted = jnp.dot(train_rows, delta, preferred_element_type=jnp.float32)]
    reshape x2 -> x0, local copies, waits for them, and re-layouts: 13.5 us -> none  [rows_of_block(): whole = whole.reshape(n_tensor, n_fsdp, share, rows)]
    psum x1 -> x0, blocking collectives: 12.6 us -> none  [per_device(): return lax.psum(partial_scores, 'tensor')]
    unnamed x1 -> x0, blocking collectives: 8.67 us -> none
  transfers between devices with their start and end apart: 4 -> 0, of which waited for: 3 -> 0; matrix products, arithmetic and copies ran while one was open for 4% -> 0% of each run, Pallas kernels for 0% -> 0%
where the time goes in v2:
time: 268 us
  Pallas kernels  267 us (100%)
    pallas_call x1, Pallas kernels, per_device(): pl.pallas_call(functools.partial(kernel, n_fsdp, n_tensor), out_shape=jax...  267 us

profile of v2, /device:TPU:0, one launch (start us, length us, event | category | flops | bytes accessed | tf_op | source)
XLA Modules:
  0.0 268.2 jit_solution(9008569782131080154)
XLA Ops:
  0.0 266.9 %scores.1 = f32[1,256]{1,0:T(1,128)} custom-call(bf16[512,1024]{1,0:T(8,128)(2,1)} %val_x.1, bf16[512,2048]{1,0:T(8,128)(2,1)} %val_cot.1, f32[2048,2048]{1,0:T(8,128)} %moment.1, bf16[256,1024]{1,0:T(8,128)(2,1)} %train_x.1, bf16[256,2048]{1,0:T(8,128)(2,1)} %train_cot.1), custom_call_target="tpu_custom_call" | custom-call | tf_op jit(solution)/shard_map/scores/pallas_call | solution.py:337
  266.9 1.2 copy.7

commit v3 on v2

v3 whole, which is shorter than its diff:
```python
import functools

import jax
import jax.numpy as jnp
from jax import lax
from jax.experimental import pallas as pl
from jax.experimental.pallas import tpu as pltpu
from jax.sharding import PartitionSpec as P

EPSILON = 1e-08
CHUNK = 256
AHEAD = 2
MESH = pl.DeviceIdType.MESH


def kernel(
    n_fsdp, n_tensor,
    val_x, val_cot, moment, train_x, train_cot, out,
    spread, spread_t, x_all, t_all, x_turned, cot, cot_t, moment_v, shifted, total,
    up_in, down_in, second,
    a_send, a_recv, b_send, b_recv, c_send, c_recv, twin_send, up_send, down_send, cot_recv,
    rise_send, rise_recv, fall_send, fall_recv,
    moment_sem, own_sem, local_sem, r2_send, r2_recv,
):
    z, t = lax.axis_index("fsdp"), lax.axis_index("tensor")
    chunks = cot.shape[0]
    depth, depth_t = val_cot.shape[0], train_cot.shape[0]
    rows, features = moment.shape[0], val_x.shape[1]
    share, share_t = spread.shape[0], spread_t.shape[0]

    def on_tensor(d):
        return lax.rem(t + d, n_tensor)

    def on_fsdp(d):
        return lax.rem(z + d, n_fsdp)

    def remote(src, dst, send, recv, device):
        return pltpu.make_async_remote_copy(
            src_ref=src, dst_ref=dst, send_sem=send, recv_sem=recv,
            device_id=device, device_id_type=MESH,
        )

    def loop(low, high, body):
        def step(i, carry):
            body(i)
            return carry
        lax.fori_loop(low, high, step, 0)

    barrier = pltpu.get_barrier_semaphore()

    @functools.partial(loop, 1, n_tensor)
    def _(d):
        pl.semaphore_signal(barrier, 1, device_id={"tensor": on_tensor(d)}, device_id_type=MESH)

    @functools.partial(loop, 1, n_fsdp)
    def _(d):
        pl.semaphore_signal(barrier, 1, device_id={"fsdp": on_fsdp(d)}, device_id_type=MESH)

    pl.semaphore_wait(barrier, n_tensor + n_fsdp - 2)

    def a_copies(peer, owner, d):
        columns = pl.ds(pl.multiple_of(owner * features, features), features)
        return (
            remote(val_x.at[pl.ds(pl.multiple_of(peer * share, share), share)],
                   spread.at[:, columns], a_send.at[0, d], a_recv.at[0, owner], {"tensor": peer}),
            remote(train_x.at[pl.ds(pl.multiple_of(peer * share_t, share_t), share_t)],
                   spread_t.at[:, columns], a_send.at[1, d], a_recv.at[1, owner], {"tensor": peer}),
        )

    def a_own():
        columns = pl.ds(pl.multiple_of(t * features, features), features)
        return (
            pltpu.make_async_copy(val_x.at[pl.ds(pl.multiple_of(t * share, share), share)],
                                  spread.at[:, columns], local_sem.at[0]),
            pltpu.make_async_copy(train_x.at[pl.ds(pl.multiple_of(t * share_t, share_t), share_t)],
                                  spread_t.at[:, columns], local_sem.at[1]),
        )

    def b_copies(peer, owner, d):
        columns = pl.ds(pl.multiple_of(peer * rows, rows), rows)
        return (
            remote(spread.at[:, columns],
                   x_all.at[owner, pl.ds(pl.multiple_of(t * share, share), share)],
                   b_send.at[0, d], b_recv.at[0, owner], {"fsdp": peer}),
            remote(spread_t.at[:, columns],
                   t_all.at[owner, pl.ds(pl.multiple_of(t * share_t, share_t), share_t)],
                   b_send.at[1, d], b_recv.at[1, owner], {"fsdp": peer}),
        )

    def b_own():
        columns = pl.ds(pl.multiple_of(z * rows, rows), rows)
        return (
            pltpu.make_async_copy(
                spread.at[:, columns],
                x_all.at[z, pl.ds(pl.multiple_of(t * share, share), share)], local_sem.at[0]),
            pltpu.make_async_copy(
                spread_t.at[:, columns],
                t_all.at[z, pl.ds(pl.multiple_of(t * share_t, share_t), share_t)],
                local_sem.at[1]),
        )

    core = lax.rem(t, 2)
    twin = t + 1 - 2 * core
    pairs = n_tensor // 2

    def same_core(d):
        return 2 * lax.rem(t // 2 + d, pairs) + core

    def c_copy(i, peer, owner, sem):
        held, size = ((x_all, share), (t_all, share_t))[i]
        piece = pl.ds(pl.multiple_of(owner * size, size), size)
        return remote(held.at[:, piece], held.at[:, piece], sem, c_recv.at[i, owner],
                      {"tensor": peer})

    def c_start(i):
        @functools.partial(loop, 1, pairs)
        def _(d):
            c_copy(i, same_core(d), t, c_send.at[i, d]).start()

        c_copy(i, twin, t, twin_send.at[i, t]).start()

    def c_pass(i):
        @functools.partial(loop, 1, pairs)
        def _(d):
            owner = same_core(d)
            c_copy(i, owner, owner, c_send.at[i, d]).wait_recv()
            c_copy(i, twin, owner, twin_send.at[i, owner]).start()

    def c_finish(i):
        @functools.partial(loop, 0, pairs)
        def _(d):
            owner = same_core(d) + 1 - 2 * core
            c_copy(i, twin, owner, twin_send.at[i, owner]).wait_recv()

    def cot_copy(shard, c, sems, peer, own):
        place = cot.at[c, pl.ds(pl.multiple_of(shard * depth, depth), depth)]
        columns = pl.ds(pl.multiple_of(c * CHUNK, CHUNK), CHUNK)
        return remote(val_cot.at[:, columns] if own else place, place,
                      sems.at[shard, c], cot_recv.at[shard, c], {"fsdp": peer})

    below, above = lax.max(z - 1, 0), lax.min(z + 1, n_fsdp - 1)

    def start_own(c):
        @pl.when(z < n_fsdp - 1)
        def _():
            cot_copy(z, c, up_send, above, True).start()

        @pl.when(z > 0)
        def _():
            cot_copy(z, c, down_send, below, True).start()

    def cot_own(c):
        columns = pl.ds(pl.multiple_of(c * CHUNK, CHUNK), CHUNK)
        place = cot.at[c, pl.ds(pl.multiple_of(z * depth, depth), depth)]
        return (
            pltpu.make_async_copy(val_cot.at[:, columns], place, own_sem.at[0, c]),
            pltpu.make_async_copy(train_cot.at[:, columns], cot_t.at[c], own_sem.at[1, c]),
        )

    def moment_copy(c):
        columns = pl.ds(pl.multiple_of(c * CHUNK, CHUNK), CHUNK)
        return pltpu.make_async_copy(moment.at[:, columns], moment_v.at[lax.rem(c, 2)],
                                     moment_sem.at[lax.rem(c, 2)])

    @functools.partial(loop, 1, n_tensor)
    def _(d):
        for copy in a_copies(on_tensor(d), t, d):
            copy.start()

    for copy in a_own():
        copy.start()
    start_own(0)

    @functools.partial(loop, 1, n_tensor)
    def _(d):
        owner = on_tensor(d)
        for copy in a_copies(owner, owner, d):
            copy.wait_recv()

    for copy in a_own():
        copy.wait()

    @functools.partial(loop, 1, n_fsdp)
    def _(d):
        for copy in b_copies(on_fsdp(d), z, d):
            copy.start()

    for copy in b_own():
        copy.start()
    loop(1, AHEAD, start_own)

    @functools.partial(loop, 0, chunks)
    def _(c):
        for copy in cot_own(c):
            copy.start()

    for c in range(2):
        moment_copy(c).start()

    @functools.partial(loop, 1, n_fsdp)
    def _(d):
        owner = on_fsdp(d)
        for copy in b_copies(owner, owner, d):
            copy.wait_recv()

    for copy in b_own():
        copy.wait()

    c_start(0)
    c_start(1)

    def pass_on(k, c):
        lower, upper = z - k, z + k

        @pl.when(lower >= 0)
        def _():
            copy = cot_copy(lower, c, up_send, above, False)
            copy.wait_recv()

            @pl.when(z < n_fsdp - 1)
            def _():
                copy.start()

        @pl.when(upper < n_fsdp)
        def _():
            copy = cot_copy(upper, c, down_send, below, False)
            copy.wait_recv()

            @pl.when(z > 0)
            def _():
                copy.start()

    tile = 256

    def turn():
        @functools.partial(loop, 0, rows // tile)
        def _(i):
            columns = pl.ds(pl.multiple_of(i * tile, tile), tile)
            for group in range(n_fsdp):
                x_turned[columns, group * depth:(group + 1) * depth] = x_all[group, :, columns].T

    def rise_copy(c, block):
        return remote(up_in.at[c, block], up_in.at[c, block],
                      rise_send.at[c, block], rise_recv.at[c, block], {"fsdp": above})

    def fall_copy(c, block):
        return remote(down_in.at[c, block], down_in.at[c, block],
                      fall_send.at[c, block], fall_recv.at[c, block], {"fsdp": below})

    def own_part(c, block):
        return shifted[c, pl.ds(pl.multiple_of(block * depth_t, depth_t), depth_t), :]

    def compute(c):
        for copy in cot_own(c):
            copy.wait()
        moment_copy(c).wait()
        shifted[c] = jnp.zeros(shifted.shape[1:], jnp.float32)

        @functools.partial(loop, 0, rows // tile)
        def _(i):
            block = pl.ds(pl.multiple_of(i * tile, tile), tile)
            grad = jnp.dot(x_turned[block, :], cot[c], preferred_element_type=jnp.float32)
            root = jnp.sqrt(moment_v[lax.rem(c, 2), block, :]) + EPSILON
            delta = (grad / root).astype(jnp.bfloat16)
            lhs = t_all[:, :, block].reshape(n_fsdp * depth_t, tile)
            shifted[c] += jnp.dot(lhs, delta, preferred_element_type=jnp.float32)

        @pl.when(c + 2 < chunks)
        def _():
            moment_copy(c + 2).start()

        @pl.when(z == 0)
        def _():
            @functools.partial(loop, 1, n_fsdp)
            def _(j):
                block = n_fsdp - j
                up_in[c, block] = own_part(c, block).astype(jnp.bfloat16)
                rise_copy(c, block).start()

        @pl.when(z == n_fsdp - 1)
        def _():
            @functools.partial(loop, 0, n_fsdp - 1)
            def _(block):
                down_in[c, block] = own_part(c, block).astype(jnp.bfloat16)
                fall_copy(c, block).start()

    def add_up(c):
        @pl.when((z > 0) & (z < n_fsdp - 1))
        def _():
            @functools.partial(loop, 1, n_fsdp)
            def _(j):
                block = n_fsdp - j

                @pl.when(block > z)
                def _():
                    copy = rise_copy(c, block)
                    copy.wait_recv()
                    summed = up_in[c, block].astype(jnp.float32) + own_part(c, block)
                    up_in[c, block] = summed.astype(jnp.bfloat16)
                    copy.start()

            @functools.partial(loop, 0, n_fsdp - 1)
            def _(block):
                @pl.when(block < z)
                def _():
                    copy = fall_copy(c, block)
                    copy.wait_recv()
                    summed = down_in[c, block].astype(jnp.float32) + own_part(c, block)
                    down_in[c, block] = summed.astype(jnp.bfloat16)
                    copy.start()

    def finish(c):
        def score(values):
            scored = values.astype(jnp.float32) * cot_t[c].astype(jnp.float32)
            for low in range(0, CHUNK, 128):
                total[...] += scored[:, low:low + 128]

        score(own_part(c, z))

        @pl.when(z > 0)
        def _():
            rise_copy(c, z).wait_recv()
            score(up_in[c, z])

        @pl.when(z < n_fsdp - 1)
        def _():
            fall_copy(c, z).wait_recv()
            score(down_in[c, z])

    total[...] = jnp.zeros_like(total)
    half = chunks // 2

    def computed(step):
        if step == chunks - 1:
            return chunks
        return max(0, min(step + 1, (step + 1 - half) * 5 // 2))

    for step in range(chunks):
        @functools.partial(loop, 1, n_fsdp)
        def _(k, step=step):
            pass_on(k, step)

        if step + AHEAD < chunks:
            start_own(step + AHEAD)
        if step == half - 1:
            c_pass(0)
        if step == half:
            c_pass(1)
            c_finish(0)
            turn()
            c_finish(1)
        done, before = computed(step - 1), computed(step - 2)
        loop(done, computed(step), compute)
        loop(before, done, add_up)
    last = computed(chunks - 2)
    loop(last, chunks, add_up)
    loop(0, chunks, finish)

    second[t] = jnp.sum(total[...].T.reshape(16, 8, depth_t), axis=0)

    def r2_copy(peer, owner, d):
        return remote(second.at[owner], second.at[owner], r2_send.at[d], r2_recv.at[owner],
                      {"tensor": peer})

    @functools.partial(loop, 1, n_tensor)
    def _(d):
        r2_copy(on_tensor(d), t, d).start()

    @functools.partial(loop, 1, n_tensor)
    def _(d):
        owner = on_tensor(d)
        r2_copy(owner, owner, d).wait_recv()

    out[...] = jnp.sum(jnp.sum(second[...], axis=0), axis=0, keepdims=True)

    @functools.partial(loop, 1, n_tensor)
    def _(d):
        peer = on_tensor(d)
        for copy in a_copies(peer, t, d) + (r2_copy(peer, t, d),):
            copy.wait_send()

    @functools.partial(loop, 1, n_fsdp)
    def _(d):
        peer = on_fsdp(d)
        for copy in b_copies(peer, z, d):
            copy.wait_send()

    for i in range(2):
        @functools.partial(loop, 1, pairs)
        def _(d, i=i):
            c_copy(i, same_core(d), t, c_send.at[i, d]).wait_send()

        @functools.partial(loop, 0, pairs)
        def _(d, i=i):
            owner = same_core(d)
            c_copy(i, twin, owner, twin_send.at[i, owner]).wait_send()

    @functools.partial(loop, 0, n_fsdp)
    def _(shard):
        @pl.when((shard <= z) & (z < n_fsdp - 1))
        def _():
            loop(0, chunks, lambda c: cot_copy(shard, c, up_send, above, False).wait_send())

        @pl.when((shard >= z) & (z > 0))
        def _():
            loop(0, chunks, lambda c: cot_copy(shard, c, down_send, below, False).wait_send())

        @pl.when(shard > z)
        def _():
            loop(0, chunks, lambda c: rise_copy(c, shard).wait_send())

        @pl.when(shard < z)
        def _():
            loop(0, chunks, lambda c: fall_copy(c, shard).wait_send())


def per_device(n_fsdp, n_tensor, val_x, val_cot, second_moment, train_x, train_cot):
    depth, depth_t = val_x.shape[0], train_x.shape[0]
    rows, hidden = second_moment.shape
    chunks = hidden // CHUNK
    width = val_x.shape[1] * n_tensor
    bf16, f32 = jnp.bfloat16, jnp.float32
    dma = pltpu.SemaphoreType.DMA
    scores = pl.pallas_call(
        functools.partial(kernel, n_fsdp, n_tensor),
        out_shape=jax.ShapeDtypeStruct((1, depth_t), f32),
        in_specs=[pl.BlockSpec(memory_space=pl.ANY)] * 5,
        out_specs=pl.BlockSpec(memory_space=pltpu.VMEM),
        scratch_shapes=[
            pltpu.VMEM((depth // n_tensor, width), bf16),
            pltpu.VMEM((depth_t // n_tensor, width), bf16),
            pltpu.VMEM((n_fsdp, depth, rows), bf16),
            pltpu.VMEM((n_fsdp, depth_t, rows), bf16),
            pltpu.VMEM((rows, n_fsdp * depth), bf16),
            pltpu.VMEM((chunks, n_fsdp * depth, CHUNK), bf16),
            pltpu.VMEM((chunks, depth_t, CHUNK), bf16),
            pltpu.VMEM((2, rows, CHUNK), f32),
            pltpu.VMEM((chunks, n_fsdp * depth_t, CHUNK), f32),
            pltpu.VMEM((depth_t, 128), f32),
            pltpu.VMEM((chunks, n_fsdp, depth_t, CHUNK), bf16),
            pltpu.VMEM((chunks, n_fsdp, depth_t, CHUNK), bf16),
            pltpu.VMEM((n_tensor, 8, depth_t), f32),
            dma((2, n_tensor)), dma((2, n_tensor)),
            dma((2, n_fsdp)), dma((2, n_fsdp)),
            dma((2, n_tensor)), dma((2, n_tensor)), dma((2, n_tensor)),
            dma((n_fsdp, chunks)), dma((n_fsdp, chunks)), dma((n_fsdp, chunks)),
            dma((chunks, n_fsdp)), dma((chunks, n_fsdp)),
            dma((chunks, n_fsdp)), dma((chunks, n_fsdp)),
            dma((2,)), dma((2, chunks)), dma((2,)),
            dma((n_tensor,)), dma((n_tensor,)),
        ],
        compiler_params=pltpu.CompilerParams(
            collective_id=0, has_side_effects=True, vmem_limit_bytes=60 * 1024 * 1024
        ),
        name="scores",
    )(val_x, val_cot, second_moment, train_x, train_cot)
    return scores.reshape(depth_t)


def solution(mesh):
    return jax.shard_map(
        functools.partial(per_device, mesh.shape["fsdp"], mesh.shape["tensor"]),
        mesh=mesh,
        in_specs=(P("fsdp", "tensor"),) * 5,
        out_specs=P("fsdp"),
        check_vma=False,
    )
```

time: 268 us -> 292 us (1.090)
  Pallas kernels: 267 us -> 290 us
    pallas_call x1, Pallas kernels: 267 us -> 290 us  [per_device(): pl.pallas_call(functools.partial(kernel, n_fsdp, n_tensor), out_shape=jax...]
where the time goes in v3:
time: 292 us
  Pallas kernels  290 us (99%)
    pallas_call x1, Pallas kernels, per_device(): pl.pallas_call(functools.partial(kernel, n_fsdp, n_tensor), out_shape=jax...  290 us

profile of v3, /device:TPU:0, one launch (start us, length us, event | category | flops | bytes accessed | tf_op | source)
XLA Modules:
  0.0 291.5 jit_solution(17676783841619091076)
XLA Ops:
  0.0 290.3 %scores.1 = f32[1,256]{1,0:T(1,128)} custom-call(bf16[512,1024]{1,0:T(8,128)(2,1)} %val_x.1, bf16[512,2048]{1,0:T(8,128)(2,1)} %val_cot.1, f32[2048,2048]{1,0:T(8,128)} %moment.1, bf16[256,1024]{1,0:T(8,128)(2,1)} %train_x.1, bf16[256,2048]{1,0:T(8,128)(2,1)} %train_cot.1), custom_call_target="tpu_custom_call" | custom-call | tf_op jit(solution)/shard_map/scores/pallas_call | solution.py:424
  290.3 1.2 copy.7

commit v4 on v3

--- a/solution.py
+++ b/solution.py
@@ -9,7 +9,6 @@
 
 EPSILON = 1e-08
 CHUNK = 256
-AHEAD = 2
 MESH = pl.DeviceIdType.MESH
 
 
@@ -187,7 +186,7 @@
 
     for copy in b_own():
         copy.start()
-    loop(1, AHEAD, start_own)
+    loop(1, chunks, start_own)
 
     @functools.partial(loop, 0, chunks)
     def _(c):
@@ -230,7 +229,7 @@
             def _():
                 copy.start()
 
-    tile = 256
+    tile = min(512, rows)
 
     def turn():
         @functools.partial(loop, 0, rows // tile)
@@ -328,32 +327,29 @@
             score(down_in[c, z])
 
     total[...] = jnp.zeros_like(total)
-    half = chunks // 2
-
-    def computed(step):
-        if step == chunks - 1:
-            return chunks
-        return max(0, min(step + 1, (step + 1 - half) * 5 // 2))
-
-    for step in range(chunks):
-        @functools.partial(loop, 1, n_fsdp)
-        def _(k, step=step):
-            pass_on(k, step)
-
-        if step + AHEAD < chunks:
-            start_own(step + AHEAD)
-        if step == half - 1:
-            c_pass(0)
-        if step == half:
-            c_pass(1)
-            c_finish(0)
-            turn()
-            c_finish(1)
-        done, before = computed(step - 1), computed(step - 2)
-        loop(done, computed(step), compute)
-        loop(before, done, add_up)
-    last = computed(chunks - 2)
-    loop(last, chunks, add_up)
+
+    loop(0, chunks, lambda c: pass_on(1, c))
+    c_pass(0)
+    c_pass(1)
+
+    @functools.partial(loop, 2, n_fsdp - 1)
+    def _(k):
+        loop(0, chunks, lambda c: pass_on(k, c))
+
+    c_finish(0)
+    c_finish(1)
+    turn()
+
+    @functools.partial(loop, 0, chunks)
+    def _(c):
+        pass_on(n_fsdp - 1, c)
+        compute(c)
+
+        @pl.when(c > 0)
+        def _():
+            add_up(c - 1)
+
+    add_up(chunks - 1)
     loop(0, chunks, finish)
 
     second[t] = jnp.sum(total[...].T.reshape(16, 8, depth_t), axis=0)

time: 292 us -> 276 us (0.945)
  Pallas kernels: 290 us -> 275 us
    pallas_call x1, Pallas kernels: 290 us -> 275 us  [per_device(): pl.pallas_call(functools.partial(kernel, n_fsdp, n_tensor), out_shape=jax...]
where the time goes in v4:
time: 276 us
  Pallas kernels  275 us (100%)
    pallas_call x1, Pallas kernels, per_device(): pl.pallas_call(functools.partial(kernel, n_fsdp, n_tensor), out_shape=jax...  275 us

profile of v4, /device:TPU:0, one launch (start us, length us, event | category | flops | bytes accessed | tf_op | source)
XLA Modules:
  0.0 275.9 jit_solution(15540404167392540630)
XLA Ops:
  0.0 274.6 %scores.1 = f32[1,256]{1,0:T(1,128)} custom-call(bf16[512,1024]{1,0:T(8,128)(2,1)} %val_x.1, bf16[512,2048]{1,0:T(8,128)(2,1)} %val_cot.1, f32[2048,2048]{1,0:T(8,128)} %moment.1, bf16[256,1024]{1,0:T(8,128)(2,1)} %train_x.1, bf16[256,2048]{1,0:T(8,128)(2,1)} %train_cot.1), custom_call_target="tpu_custom_call" | custom-call | tf_op jit(solution)/shard_map/scores/pallas_call | solution.py:420
  274.6 1.2 copy.7
